TPU v7x, 32 devices: a whole 2x2x4 slice. The times are simulated.
32 devices in a mesh: space: 8 (over y, x, core), orb: 4 (over z).
Axes of the slice: x: 2, y: 2, z: 4, core: 2. Of those that a mesh axis runs over, the one named last changes fastest.
Arguments:
- orbitals: float32 [64, 16, 32, 512], P('space', None, None, 'orb'), may hold values from -75 to 75
- potential: float32 [64, 16, 32], P('space'), may hold values from -2 to 0
Outputs:
- whitened: float32 [64, 16, 32, 512], P('space', None, None, 'orb')
All inputs are finite; a program needn't handle non-finite values.
Results may differ from a plain program's by a relative error of at most 0.0003.
Values sent between devices are 32-bit elements; how exact they have to be, the bound alone decides.
A program may use at most 192 MiB of HBM per device.

v0:
```python
import jax
import jax.numpy as jnp
from jax import lax
from jax.sharding import PartitionSpec as P

DEGREE = 4
NS_ITERS = 8


STENCIL_WEIGHTS = [-49.0 / 18.0, 3.0 / 2.0, -3.0 / 20.0, 1.0 / 90.0]
CENTER = 5.0
HALF_WIDTH = 4.0


def padded_2(cells, sides, width):
    for axis, dim in sides:
        count = lax.axis_size(axis)
        head = lax.slice_in_dim(cells, 0, width, axis=dim)
        tail = lax.slice_in_dim(cells, cells.shape[dim] - width, cells.shape[dim], axis=dim)
        cells = jnp.concatenate(
            [
                lax.ppermute(tail, axis, [(i, (i + 1) % count) for i in range(count)]),
                cells,
                lax.ppermute(head, axis, [((i + 1) % count, i) for i in range(count)]),
            ],
            axis=dim,
        )
    return cells


def slab_hamiltonian(field, potential):
    padded = padded_2(field, (("space", 0),), 3)
    planes = field.shape[0]
    laplace = 3.0 * STENCIL_WEIGHTS[0] * field
    for offset in range(1, 4):
        along_first = (
            padded[3 + offset : 3 + offset + planes] + padded[3 - offset : 3 - offset + planes]
        )
        along_second = jnp.roll(field, offset, 1) + jnp.roll(field, -offset, 1)
        along_third = jnp.roll(field, offset, 2) + jnp.roll(field, -offset, 2)
        laplace = laplace + STENCIL_WEIGHTS[offset] * (along_first + along_second + along_third)
    return -0.5 * laplace + potential[..., None] * field


def chebyshev(start, apply_operator):
    previous = start
    current = (apply_operator(start) - CENTER * start) / HALF_WIDTH
    for degree_step in range(2, DEGREE + 1):
        following = 2.0 * (apply_operator(current) - CENTER * current) / HALF_WIDTH - previous
        previous = current
        current = following
    return current


def whiten_factor(intersection):
    norm_scale = jnp.sqrt(jnp.sum(intersection * intersection) + 1e-06)
    identity = jnp.eye(intersection.shape[0], dtype=jnp.float32)
    scaled = intersection / norm_scale
    inverse = identity
    for step in range(NS_ITERS):
        factor = 1.5 * identity - 0.5 * jnp.dot(inverse, scaled, precision=lax.Precision.HIGHEST)
        scaled = jnp.dot(scaled, factor, precision=lax.Precision.HIGHEST)
        inverse = jnp.dot(factor, inverse, precision=lax.Precision.HIGHEST)
    return inverse / jnp.sqrt(norm_scale)


def body(orbitals, potential):
    local_orbs = orbitals.shape[-1]

    def slab_operator(field):
        return slab_hamiltonian(field, potential)

    filtered = chebyshev(orbitals, slab_operator)
    cell_rows = filtered.reshape(-1, local_orbs)
    total_cells = cell_rows.shape[0] * lax.axis_size("space")
    gathered = lax.all_gather(cell_rows, "orb", axis=1, tiled=True)
    partial_terms = jnp.dot(gathered.T, gathered, precision=lax.Precision.HIGHEST)
    intersection = lax.psum(partial_terms, "space") / total_cells
    root_inverse = whiten_factor(intersection)
    start = lax.axis_index("orb") * local_orbs
    own_columns = lax.dynamic_slice_in_dim(root_inverse, start, local_orbs, 1)
    whitened = jnp.dot(gathered, own_columns, precision=lax.Precision.HIGHEST)
    return whitened.reshape(filtered.shape)


def solution(mesh):
    return jax.shard_map(
        body,
        mesh=mesh,
        in_specs=(P("space", None, None, "orb"), P("space", None, None)),
        out_specs=P("space", None, None, "orb"),
        check_vma=False,
    )
```

profile of v0, /device:TPU:0, one launch (start us, length us, event | category | flops | bytes accessed | tf_op | source)
XLA Modules:
  0.0 439.6 jit_solution(12899655219555692049)
XLA Ops:
  6.5 1.7 fusion.142
  8.7 2.9 collective-permute-start
  12.6 1.8 fusion.135
  14.5 1.8 fusion.139
  16.3 2.3 fusion.144
  18.7 0.7 fusion.138
  19.5 0.8 fusion.140
  20.9 0.7 fusion.134
  22.3 4.7 %collective-permute-done.1 = f32[3,16,32,128]{3,2,1,0:T(8,128)S(1)} collective-permute-done((f32[3,16,32,128]{3,2,1,0:T(8,128)S(1)}, f32[3,16,32,128]{3,2,1,0:T(8,128)S(1)}, u32[]{:S(2)}, u32[]{:S(2)}) %collective-permute-start.1) | collective-permute-done | bytes 786464 | tf_op jit(solution)/shard_map/ppermute | solution.py:22
  27.7 0.9 collective-permute-done
  28.6 7.3 %broadcast_multiply_fusion = (f32[8,16,32,128]{3,2,1,0:T(8,128)S(1)}, f32[8,16,32,128]{3,2,1,0:T(8,128)S(1)}) fusion(f32[8,16,32,128]{3,2,1,0:T(8,128)S(1)} %copy-done, f32[8,16,32]{2,1,0:T(8,128)S(1)} %copy-done.1, f32[8,16,3,128]{3,2,1,0:T(4,128)S(1)} %get-tuple-element.110, f32[8,16,29,128]{3,2,1,0:T(8,128)S(1)} %get-tuple-element.112, ...), kind=kLoop, calls=%fused_computation.163 | loop fusion | flops 20971520 | bytes 44056576 | tf_op jit(solution)/shard_map/div | solution.py:47
  36.6 1.8 fusion.131
  38.4 2.4 fusion.127
  40.9 2.2 fusion.123
  43.7 2.9 collective-permute-start.2
  47.9 16.6 %collective-permute-done.2 = f32[3,16,32,128]{3,2,1,0:T(8,128)S(1)} collective-permute-done((f32[3,16,32,128]{3,2,1,0:T(8,128)S(1)}, f32[3,16,32,128]{3,2,1,0:T(8,128)S(1)}, u32[]{:S(2)}, u32[]{:S(2)}) %collective-permute-start.2) | collective-permute-done | bytes 786464 | tf_op jit(solution)/shard_map/ppermute | solution.py:24
  66.0 9.3 %fusion.51 = f32[8,16,32,128]{3,2,1,0:T(8,128)S(1)} fusion(f32[8,16,32,128]{3,2,1,0:T(8,128)S(1)} %copy-done, f32[8,16,32,128]{3,2,1,0:T(8,128)S(1)} %get-tuple-element.5, f32[3,16,32,128]{3,2,1,0:T(8,128)} %copy-done.6, f32[3,16,32,128]{3,2,1,0:T(8,128)} %copy-done.3, f32[8,15,32,128]{3,2,1,0:T(8,128)} %get-tuple-element.80, ...), kind=kLoop, calls=%fused_computation.83 | loop fusion | flops 24641536 | bytes 35143680 | tf_op jit(solution)/shard_map/sub | solution.py:49
  76.6 1.8 fusion.114
  78.3 2.3 fusion.110
  80.9 0.8 fusion.109
  81.7 0.9 fusion.115
  82.6 0.8 fusion.113
  83.4 0.7 fusion.117
  84.1 2.5 collective-permute-start.4
  88.9 14.8 %collective-permute-done.4 = f32[3,16,32,128]{3,2,1,0:T(8,128)S(1)} collective-permute-done((f32[3,16,32,128]{3,2,1,0:T(8,128)S(1)}, f32[3,16,32,128]{3,2,1,0:T(8,128)S(1)}, u32[]{:S(2)}, u32[]{:S(2)}) %collective-permute-start.4) | collective-permute-done | bytes 786464 | tf_op jit(solution)/shard_map/ppermute | solution.py:24
  103.6 0.9 copy-done.5
  104.8 9.4 %fusion.31 = f32[8,16,32,128]{3,2,1,0:T(8,128)S(1)} fusion(f32[8,16,32,128]{3,2,1,0:T(8,128)S(1)} %fusion.51, f32[3,16,32,128]{3,2,1,0:T(8,128)} %copy-done.8, f32[3,16,32,128]{3,2,1,0:T(8,128)} %copy-done.5, f32[8,15,32,128]{3,2,1,0:T(8,128)S(1)} %get-tuple-element.54, f32[8,1,32,128]{3,2,1,0:T(8,128)} %get-tuple-element.56, ...), kind=kLoop, calls=%fused_computation.63 | loop fusion | flops 25165824 | bytes 33046528 | tf_op jit(solution)/shard_map/sub | solution.py:49
  116.0 2.3 fusion.97
  118.6 0.9 fusion.102
  119.5 0.8 fusion.100
  120.3 0.7 fusion.104
  121.0 2.8 collective-permute-start.6
  125.9 13.8 %collective-permute-done.6 = f32[3,16,32,128]{3,2,1,0:T(8,128)S(1)} collective-permute-done((f32[3,16,32,128]{3,2,1,0:T(8,128)S(1)}, f32[3,16,32,128]{3,2,1,0:T(8,128)S(1)}, u32[]{:S(2)}, u32[]{:S(2)}) %collective-permute-start.6) | collective-permute-done | bytes 786464 | tf_op jit(solution)/shard_map/ppermute | solution.py:24
  139.7 1.0 collective-permute-done.7
  140.7 0.9 copy-done.7
  141.6 10.1 %fusion.11 = f32[8,16,32,128]{3,2,1,0:T(8,128)} fusion(f32[8,16,32,128]{3,2,1,0:T(8,128)S(1)} %fusion.51, f32[8,16,32,128]{3,2,1,0:T(8,128)S(1)} %fusion.31, f32[3,16,32,128]{3,2,1,0:T(8,128)} %copy-done.7, f32[3,16,32,128]{3,2,1,0:T(8,128)} %copy-done.4, f32[8,15,32,128]{3,2,1,0:T(8,128)S(1)} %get-tuple-element.28, f32[8,1,32,128]{3,2,1,0:T(8,128)} %get-tuple-element.30, ...), kind=kLoop, calls=%fused_computation.43 | loop fusion | flops 24641536 | bytes 33046528 | tf_op jit(solution)/shard_map/sub | solution.py:49
  151.7 150.8 %all-gather.2.cloned.1.call-done = f32[4096,512]{1,0:T(8,128)} async-done(((f32[4096,128]{1,0:T(8,128)}), f32[4096,512]{1,0:T(8,128)}) %all-gather.2.cloned.1.call-update) | async-done | bytes 8388624 | tf_op jit(solution)/shard_map/all_gather | solution.py:76
  302.5 18.7 %fusion.147 = f32[512,512]{1,0:T(8,128)} fusion(f32[4096,512]{1,0:T(8,128)} %all-gather.2.cloned.1.call-done), kind=kOutput, calls=%fused_computation.229 | convolution fusion | flops 12884901888 | bytes 9437184 | tf_op jit(solution)/shard_map/dot_general | solution.py:77
  321.2 54.9 %all-reduce.2.cloned.1.call-done = f32[512,512]{1,0:T(8,128)} async-done(((f32[512,512]{1,0:T(8,128)}), f32[512,512]{1,0:T(8,128)}) %all-reduce.2.cloned.1.call-update) | async-done | bytes 1048592 | tf_op jit(solution)/shard_map/psum | solution.py:78
  376.1 2.1 multiply_reduce_fusion
  378.9 2.3 select_subtract_fusion.7
  381.3 1.0 fusion.87
  382.5 1.9 fusion.88
  384.4 1.9 select_subtract_fusion.6
  386.2 1.8 fusion.149
  388.1 1.8 fusion.148
  389.9 1.8 select_subtract_fusion.5
  391.8 2.0 fusion.151
  393.8 1.8 fusion.150
  395.7 1.9 select_subtract_fusion.4
  397.6 1.8 fusion.153
  399.4 1.8 fusion.152
  401.3 1.9 select_subtract_fusion.3
  403.1 1.8 fusion.155
  405.0 2.1 fusion.154
  407.1 1.8 select_subtract_fusion.2
  408.9 1.8 fusion.157
  410.8 1.8 fusion.156
  412.6 1.8 select_subtract_fusion.1
  414.5 1.8 fusion.159
  416.3 1.8 fusion.158
  418.2 2.1 select_subtract_fusion
  420.4 1.8 fusion.160
  422.2 10.1 %fusion.89 = f32[4096,128]{1,0:T(8,128)} fusion(f32[4096,512]{1,0:T(8,128)} %all-gather.2.cloned.1.call-done, f32[512,512]{1,0:T(8,128)S(1)} %fusion.160, s32[]{:T(128)S(6)} %select_n.3, f32[]{:T(128)S(6)} %sqrt.7), kind=kOutput, calls=%fused_computation.167 | convolution fusion | flops 3221291008 | bytes 10747912 | tf_op jit(solution)/shard_map/dot_general | solution.py:82
  (62 shorter events, 16.0 us)
Async XLA Ops:
  6.5 5.1 %copy-start = (f32[8,16,32,128]{3,2,1,0:T(8,128)S(1)}, f32[8,16,32,128]{3,2,1,0:T(8,128)}, u32[]{:S(2)}) copy-start(f32[8,16,32,128]{3,2,1,0:T(8,128)} %param.2) | copy-start | bytes 6291460
  6.5 295.9 %all-gather.2.cloned.1.call-start = ((), (), s32[]{:S(2)}) async-start(), calls=%async_computation | async-start | bytes 10485760 | tf_op jit(solution)/shard_map/all_gather | solution.py:76
  8.2 18.8 %collective-permute-start.1 = (f32[3,16,32,128]{3,2,1,0:T(8,128)S(1)}, f32[3,16,32,128]{3,2,1,0:T(8,128)S(1)}, u32[]{:S(2)}, u32[]{:S(2)}) collective-permute-start(f32[3,16,32,128]{3,2,1,0:T(8,128)S(1)} %get-tuple-element.102), channel_id=1, source_target_pairs={{0,4},{4,8},{8,12},{12,16},{16,20},{20,24},{24,28},{28,0},{1,5},{5... | collective-permute-start | bytes 2359304 | tf_op jit(solution)/shard_map/ppermute | solution.py:22
  8.7 19.8 %collective-permute-start = (f32[3,16,32,128]{3,2,1,0:T(8,128)S(1)}, f32[3,16,32,128]{3,2,1,0:T(8,128)S(1)}, u32[]{:S(2)}, u32[]{:S(2)}) collective-permute-start(f32[3,16,32,128]{3,2,1,0:T(8,128)S(1)} %get-tuple-element.101), channel_id=1, source_target_pairs={{4,0},{8,4},{12,8},{16,12},{20,16},{24,20},{28,24},{0,28},{5,1},{9... | collective-permute-start | bytes 2359304 | tf_op jit(solution)/shard_map/ppermute | solution.py:24
  18.6 3.1 copy-start.1
  43.7 20.8 %collective-permute-start.2 = (f32[3,16,32,128]{3,2,1,0:T(8,128)S(1)}, f32[3,16,32,128]{3,2,1,0:T(8,128)S(1)}, u32[]{:S(2)}, u32[]{:S(2)}) collective-permute-start(f32[3,16,32,128]{3,2,1,0:T(8,128)S(1)} %get-tuple-element.83), channel_id=1, source_target_pairs={{4,0},{8,4},{12,8},{16,12},{20,16},{24,20},{28,24},{0,28},{5,1},{9... | collective-permute-start | bytes 2359304 | tf_op jit(solution)/shard_map/ppermute | solution.py:24
  46.6 18.5 %collective-permute-start.3 = (f32[3,16,32,128]{3,2,1,0:T(8,128)S(1)}, f32[3,16,32,128]{3,2,1,0:T(8,128)S(1)}, u32[]{:S(2)}, u32[]{:S(2)}) collective-permute-start(f32[3,16,32,128]{3,2,1,0:T(8,128)S(1)} %get-tuple-element.84), channel_id=1, source_target_pairs={{0,4},{4,8},{8,12},{12,16},{16,20},{20,24},{24,28},{28,0},{1,5},{5... | collective-permute-start | bytes 2359304 | tf_op jit(solution)/shard_map/ppermute | solution.py:22
  64.5 0.9 copy-start.3
  65.1 1.0 copy-start.6
  84.1 19.5 %collective-permute-start.4 = (f32[3,16,32,128]{3,2,1,0:T(8,128)S(1)}, f32[3,16,32,128]{3,2,1,0:T(8,128)S(1)}, u32[]{:S(2)}, u32[]{:S(2)}) collective-permute-start(f32[3,16,32,128]{3,2,1,0:T(8,128)S(1)} %get-tuple-element.57), channel_id=1, source_target_pairs={{4,0},{8,4},{12,8},{16,12},{20,16},{24,20},{28,24},{0,28},{5,1},{9... | collective-permute-start | bytes 2359304 | tf_op jit(solution)/shard_map/ppermute | solution.py:24
  86.6 17.0 %collective-permute-start.5 = (f32[3,16,32,128]{3,2,1,0:T(8,128)S(1)}, f32[3,16,32,128]{3,2,1,0:T(8,128)S(1)}, u32[]{:S(2)}, u32[]{:S(2)}) collective-permute-start(f32[3,16,32,128]{3,2,1,0:T(8,128)S(1)} %get-tuple-element.58), channel_id=1, source_target_pairs={{0,4},{4,8},{8,12},{12,16},{16,20},{20,24},{24,28},{28,0},{1,5},{5... | collective-permute-start | bytes 2359304 | tf_op jit(solution)/shard_map/ppermute | solution.py:22
  103.6 0.9 copy-start.5
  103.6 1.2 copy-start.8
  121.0 18.6 %collective-permute-start.6 = (f32[3,16,32,128]{3,2,1,0:T(8,128)S(1)}, f32[3,16,32,128]{3,2,1,0:T(8,128)S(1)}, u32[]{:S(2)}, u32[]{:S(2)}) collective-permute-start(f32[3,16,32,128]{3,2,1,0:T(8,128)S(1)} %get-tuple-element.31), channel_id=1, source_target_pairs={{4,0},{8,4},{12,8},{16,12},{20,16},{24,20},{28,24},{0,28},{5,1},{9... | collective-permute-start | bytes 2359304 | tf_op jit(solution)/shard_map/ppermute | solution.py:24
  123.9 16.8 %collective-permute-start.7 = (f32[3,16,32,128]{3,2,1,0:T(8,128)S(1)}, f32[3,16,32,128]{3,2,1,0:T(8,128)S(1)}, u32[]{:S(2)}, u32[]{:S(2)}) collective-permute-start(f32[3,16,32,128]{3,2,1,0:T(8,128)S(1)} %get-tuple-element.32), channel_id=1, source_target_pairs={{0,4},{4,8},{8,12},{12,16},{16,20},{20,24},{24,28},{28,0},{1,5},{5... | collective-permute-start | bytes 2359304 | tf_op jit(solution)/shard_map/ppermute | solution.py:22
  139.7 1.0 copy-start.4
  140.7 0.9 copy-start.7
  151.7 224.4 %all-reduce.2.cloned.1.call-start = ((), (), s32[]{:S(2)}) async-start(), calls=%async_computation.1 | async-start | bytes 2097152 | tf_op jit(solution)/shard_map/psum | solution.py:78
  381.2 1.2 copy-start.2
Sparse Core Ops, SparseCore 0:
  151.8 150.6 all-gather.1
  321.3 54.7 all-reduce.1
where the time goes:
time: 448 us; the launch traced here: 440 us
  waiting for transfers between devices  258 us (58%)
  matrix products  71.6 us (16%)
  local copies, waits for them, and re-layouts  44.7 us (10%)
  other arithmetic  38.2 us (9%)
  between operations  15.1 us (3%)
  starting transfers between devices  11.9 us (3%)
    all_gather x1, waiting for transfers between devices, body(): gathered = lax.all_gather(cell_rows, 'orb', axis=1, tiled=True)  151 us
    psum x1, waiting for transfers between devices, body(): intersection = lax.psum(partial_terms, 'space') / total_cells  54.9 us
    ppermute x4, waiting for transfers between devices, padded_2(): lax.ppermute(head, axis, [((i + 1) % count, i) for i in range(count)])  46.1 us
    sub x3, other arithmetic, chebyshev(): 2.0 * (apply_operator(current) - CENTER * current) / HALF_WIDTH - previous  28.8 us
    slice x24, local copies, waits for them, and re-layouts, slab_hamiltonian(): along_second = jnp.roll(field, offset, 1) + jnp.roll(field, -offset, 1)  25.3 us
    dot_general x1, matrix products, body(): jnp.dot(gathered.T, gathered, precision=lax.Precision.HIGHEST)  18.7 us
    dot_general x8, matrix products, whiten_factor(): jnp.dot(inverse, scaled, precision=lax.Precision.HIGHEST)  15.5 us
    dot_general x8, matrix products, whiten_factor(): inverse = jnp.dot(factor, inverse, precision=lax.Precision.HIGHEST)  14.1 us
  transfers between devices with their start and end apart: 10, of which 9 were waited for; matrix products, arithmetic and copies ran while one was open for 4% of the time, Pallas kernels for 0%

commit v1 on v0

--- a/solution.py
+++ b/solution.py
@@ -52,15 +52,21 @@
     return current
 
 
+def product(left, right):
+    return jnp.dot(left, right, precision=lax.Precision.HIGH)
+
+
 def whiten_factor(intersection):
     norm_scale = jnp.sqrt(jnp.sum(intersection * intersection) + 1e-06)
     identity = jnp.eye(intersection.shape[0], dtype=jnp.float32)
     scaled = intersection / norm_scale
-    inverse = identity
-    for step in range(NS_ITERS):
-        factor = 1.5 * identity - 0.5 * jnp.dot(inverse, scaled, precision=lax.Precision.HIGHEST)
-        scaled = jnp.dot(scaled, factor, precision=lax.Precision.HIGHEST)
-        inverse = jnp.dot(factor, inverse, precision=lax.Precision.HIGHEST)
+    inverse = 1.5 * identity - 0.5 * scaled
+    scaled = product(scaled, inverse)
+    for step in range(1, NS_ITERS):
+        factor = 1.5 * identity - 0.5 * product(inverse, scaled)
+        if step < NS_ITERS - 1:
+            scaled = product(scaled, factor)
+        inverse = product(factor, inverse)
     return inverse / jnp.sqrt(norm_scale)
 
 
@@ -73,13 +79,11 @@
     filtered = chebyshev(orbitals, slab_operator)
     cell_rows = filtered.reshape(-1, local_orbs)
     total_cells = cell_rows.shape[0] * lax.axis_size("space")
-    gathered = lax.all_gather(cell_rows, "orb", axis=1, tiled=True)
-    partial_terms = jnp.dot(gathered.T, gathered, precision=lax.Precision.HIGHEST)
-    intersection = lax.psum(partial_terms, "space") / total_cells
-    root_inverse = whiten_factor(intersection)
-    start = lax.axis_index("orb") * local_orbs
-    own_columns = lax.dynamic_slice_in_dim(root_inverse, start, local_orbs, 1)
-    whitened = jnp.dot(gathered, own_columns, precision=lax.Precision.HIGHEST)
+    mixed = lax.all_to_all(cell_rows, "orb", split_axis=0, concat_axis=1, tiled=True)
+    partial_terms = product(mixed.T, mixed)
+    intersection = lax.psum(partial_terms, ("space", "orb")) / total_cells
+    whitened = product(mixed, whiten_factor(intersection))
+    whitened = lax.all_to_all(whitened, "orb", split_axis=1, concat_axis=0, tiled=True)
     return whitened.reshape(filtered.shape)
 
 

time: 448 us -> 435 us (0.971)
  blocking collectives: 0 us -> 101 us
  waiting for transfers between devices: 258 us -> 178 us
  matrix products: 71.6 us -> 31.2 us
  local copies, waits for them, and re-layouts: 44.7 us -> 52.7 us
    all_gather x1 -> x0, waiting for transfers between devices: 151 us -> none  [body(): gathered = lax.all_gather(cell_rows, 'orb', axis=1, tiled=True)]
    all_to_all x0 -> x2, blocking collectives: none -> 101 us  [the longest x1 50.5 us: body(): lax.all_to_all(cell_rows, 'orb', split_axis=0, concat_axis=1, tiled=True)]
    psum x1, waiting for transfers between devices: 54.9 us -> 126 us  [body(): intersection = lax.psum(partial_terms, ('space', 'orb')) / total_cells]
    dot_general x25 -> x23, matrix products: 71.6 us -> 31.2 us  [product(): return jnp.dot(left, right, precision=lax.Precision.HIGH)]
    all_to_all x0 -> x2, local copies, waits for them, and re-layouts: none -> 4.97 us  [body(): lax.all_to_all(cell_rows, 'orb', split_axis=0, concat_axis=1, tiled=True)]
  transfers between devices with their start and end apart: 10 -> 9, of which waited for: 9 -> 8; matrix products, arithmetic and copies ran while one was open for 4% -> 5% of each run, Pallas kernels for 0% -> 0%
where the time goes in v1:
time: 435 us; the launch traced here: 427 us
  waiting for transfers between devices  178 us (41%)
  blocking collectives  101 us (23%)
  local copies, waits for them, and re-layouts  52.7 us (12%)
  other arithmetic  37.5 us (9%)
  matrix products  31.2 us (7%)
  between operations  15.1 us (3%)
  starting transfers between devices  11.8 us (3%)
    psum x1, waiting for transfers between devices, body(): intersection = lax.psum(partial_terms, ('space', 'orb')) / total_cells  126 us
    all_to_all x1, blocking collectives, body(): lax.all_to_all(cell_rows, 'orb', split_axis=0, concat_axis=1, tiled=True)  50.5 us
    all_to_all x1, blocking collectives, body(): lax.all_to_all(whitened, 'orb', split_axis=1, concat_axis=0, tiled=True)  50.1 us
    ppermute x4, waiting for transfers between devices, padded_2(): lax.ppermute(head, axis, [((i + 1) % count, i) for i in range(count)])  46 us
    dot_general x23, matrix products, product(): return jnp.dot(left, right, precision=lax.Precision.HIGH)  31.2 us
    sub x3, other arithmetic, chebyshev(): 2.0 * (apply_operator(current) - CENTER * current) / HALF_WIDTH - previous  28.1 us
    slice x24, local copies, waits for them, and re-layouts, slab_hamiltonian(): along_second = jnp.roll(field, offset, 1) + jnp.roll(field, -offset, 1)  26.4 us
    slice x24, local copies, waits for them, and re-layouts, slab_hamiltonian(): along_third = jnp.roll(field, offset, 2) + jnp.roll(field, -offset, 2)  14 us
  transfers between devices with their start and end apart: 9, of which 8 were waited for; matrix products, arithmetic and copies ran while one was open for 5% of the time, Pallas kernels for 0%

profile of v1, /device:TPU:0, one launch (start us, length us, event | category | flops | bytes accessed | tf_op | source)
XLA Modules:
  0.0 427.1 jit_solution(9769058541664698278)
XLA Ops:
  6.5 1.7 fusion.158
  8.7 2.9 collective-permute-start
  12.6 1.8 fusion.151
  14.5 1.8 fusion.155
  16.3 2.3 fusion.160
  19.5 0.8 fusion.156
  22.3 4.7 %collective-permute-done.1 = f32[3,16,32,128]{3,2,1,0:T(8,128)S(1)} collective-permute-done((f32[3,16,32,128]{3,2,1,0:T(8,128)S(1)}, f32[3,16,32,128]{3,2,1,0:T(8,128)S(1)}, u32[]{:S(2)}, u32[]{:S(2)}) %collective-permute-start.1) | collective-permute-done | bytes 786464 | tf_op jit(solution)/shard_map/ppermute | solution.py:22
  27.7 0.9 collective-permute-done
  28.6 7.3 %broadcast_multiply_fusion = (f32[8,16,32,128]{3,2,1,0:T(8,128)S(1)}, f32[8,16,32,128]{3,2,1,0:T(8,128)S(1)}) fusion(f32[8,16,32,128]{3,2,1,0:T(8,128)S(1)} %copy-done, f32[8,16,32]{2,1,0:T(8,128)S(1)} %copy-done.2, f32[8,16,3,128]{3,2,1,0:T(4,128)S(1)} %get-tuple-element.110, f32[8,16,29,128]{3,2,1,0:T(8,128)S(1)} %get-tuple-element.112, ...), kind=kLoop, calls=%fused_computation.167 | loop fusion | flops 20971520 | bytes 44056576 | tf_op jit(solution)/shard_map/div | solution.py:47
  36.6 1.8 fusion.147
  38.4 2.4 fusion.143
  40.8 2.2 fusion.139
  43.7 2.9 collective-permute-start.2
  47.9 16.6 %collective-permute-done.2 = f32[3,16,32,128]{3,2,1,0:T(8,128)S(1)} collective-permute-done((f32[3,16,32,128]{3,2,1,0:T(8,128)S(1)}, f32[3,16,32,128]{3,2,1,0:T(8,128)S(1)}, u32[]{:S(2)}, u32[]{:S(2)}) %collective-permute-start.2) | collective-permute-done | bytes 786464 | tf_op jit(solution)/shard_map/ppermute | solution.py:24
  66.0 9.3 %fusion.51 = f32[8,16,32,128]{3,2,1,0:T(8,128)S(1)} fusion(f32[8,16,32,128]{3,2,1,0:T(8,128)S(1)} %copy-done, f32[8,16,32,128]{3,2,1,0:T(8,128)S(1)} %get-tuple-element.5, f32[3,16,32,128]{3,2,1,0:T(8,128)} %copy-done.7, f32[3,16,32,128]{3,2,1,0:T(8,128)} %copy-done.4, f32[8,15,32,128]{3,2,1,0:T(8,128)} %get-tuple-element.80, ...), kind=kLoop, calls=%fused_computation.83 | loop fusion | flops 24641536 | bytes 35143680 | tf_op jit(solution)/shard_map/sub | solution.py:49
  76.6 1.8 fusion.130
  78.3 2.3 fusion.126
  80.9 0.8 fusion.125
  81.7 0.9 fusion.131
  82.5 0.8 fusion.129
  84.1 2.5 collective-permute-start.4
  88.8 14.8 %collective-permute-done.4 = f32[3,16,32,128]{3,2,1,0:T(8,128)S(1)} collective-permute-done((f32[3,16,32,128]{3,2,1,0:T(8,128)S(1)}, f32[3,16,32,128]{3,2,1,0:T(8,128)S(1)}, u32[]{:S(2)}, u32[]{:S(2)}) %collective-permute-start.4) | collective-permute-done | bytes 786464 | tf_op jit(solution)/shard_map/ppermute | solution.py:24
  103.6 0.9 copy-done.6
  104.7 9.4 %fusion.31 = f32[8,16,32,128]{3,2,1,0:T(8,128)S(1)} fusion(f32[8,16,32,128]{3,2,1,0:T(8,128)S(1)} %fusion.51, f32[3,16,32,128]{3,2,1,0:T(8,128)} %copy-done.9, f32[3,16,32,128]{3,2,1,0:T(8,128)} %copy-done.6, f32[8,15,32,128]{3,2,1,0:T(8,128)S(1)} %get-tuple-element.54, f32[8,1,32,128]{3,2,1,0:T(8,128)} %get-tuple-element.56, ...), kind=kLoop, calls=%fused_computation.63 | loop fusion | flops 25165824 | bytes 33046528 | tf_op jit(solution)/shard_map/sub | solution.py:49
  115.4 1.8 fusion.117
  117.1 2.3 fusion.113
  119.7 0.8 fusion.112
  120.5 0.9 fusion.118
  121.4 0.8 fusion.116
  122.9 2.8 collective-permute-start.6
  127.7 13.8 %collective-permute-done.6 = f32[3,16,32,128]{3,2,1,0:T(8,128)S(1)} collective-permute-done((f32[3,16,32,128]{3,2,1,0:T(8,128)S(1)}, f32[3,16,32,128]{3,2,1,0:T(8,128)S(1)}, u32[]{:S(2)}, u32[]{:S(2)}) %collective-permute-start.6) | collective-permute-done | bytes 786464 | tf_op jit(solution)/shard_map/ppermute | solution.py:24
  141.5 1.0 collective-permute-done.7
  142.5 0.9 copy-done.8
  143.4 9.4 %fusion.11 = f32[8,16,32,128]{3,2,1,0:T(8,128)S(1)} fusion(f32[8,16,32,128]{3,2,1,0:T(8,128)S(1)} %fusion.51, f32[8,16,32,128]{3,2,1,0:T(8,128)S(1)} %fusion.31, f32[3,16,32,128]{3,2,1,0:T(8,128)} %copy-done.8, f32[3,16,32,128]{3,2,1,0:T(8,128)} %copy-done.5, f32[8,15,32,128]{3,2,1,0:T(8,128)S(1)} %get-tuple-element.28, ...), kind=kLoop, calls=%fused_computation.43 | loop fusion | flops 24641536 | bytes 33046528 | tf_op jit(solution)/shard_map/sub | solution.py:49
  152.8 50.5 %all_to_all.32 = f32[4,1024,128]{2,1,0:T(8,128)S(1)} all-to-all(f32[4,1024,128]{2,1,0:T(8,128)S(1)} %bitcast.53), channel_id=1, replica_groups=mesh['space'=8,'orb'=4] {'orb'}, dimensions={0} | all-to-all | bytes 4194304 | tf_op jit(solution)/shard_map/all_to_all | solution.py:82
  203.3 2.8 fusion.60
  206.1 2.7 copy.4
  208.8 2.3 reshape.15
  211.1 125.9 %all-reduce.2.cloned.1.call-done = f32[512,512]{1,0:T(8,128)} async-done(((f32[512,512]{1,0:T(8,128)}), f32[512,512]{1,0:T(8,128)}) %all-reduce.2.cloned.1.call-update) | async-done | bytes 1048592 | tf_op jit(solution)/shard_map/psum | solution.py:84
  337.0 2.1 multiply_reduce_fusion
  339.8 2.9 fusion.91
  342.6 1.0 select_subtract_fusion.6
  343.7 1.0 fusion.163
  344.7 1.1 fusion.90
  345.8 1.0 select_subtract_fusion.5
  346.8 1.0 fusion.165
  347.8 1.0 fusion.164
  348.8 1.0 select_subtract_fusion.4
  349.8 1.0 fusion.167
  350.9 1.0 fusion.166
  351.9 1.0 select_subtract_fusion.3
  352.9 1.0 fusion.169
  353.9 1.3 fusion.168
  355.2 1.0 select_subtract_fusion.2
  356.2 1.0 fusion.171
  357.2 1.0 fusion.170
  358.2 1.0 select_subtract_fusion.1
  359.2 1.0 fusion.173
  360.2 2.0 fusion.172
  362.3 2.3 select_subtract_fusion
  364.6 1.9 convolution_divide_fusion
  366.5 1.9 fusion.174
  368.4 50.1 %all_to_all.33 = f32[1024,4,128]{2,0,1:T(8,128)S(1)} all-to-all(f32[1024,4,128]{2,0,1:T(8,128)S(1)} %fusion.174), channel_id=1, replica_groups=mesh['space'=8,'orb'=4] {'orb'}, dimensions={1} | all-to-all | bytes 4194304 | tf_op jit(solution)/shard_map/all_to_all | solution.py:86
  418.5 1.3 copy.14
  (64 shorter events, 17.9 us)
Async XLA Ops:
  6.5 5.1 %copy-start = (f32[8,16,32,128]{3,2,1,0:T(8,128)S(1)}, f32[8,16,32,128]{3,2,1,0:T(8,128)}, u32[]{:S(2)}) copy-start(f32[8,16,32,128]{3,2,1,0:T(8,128)} %param.2) | copy-start | bytes 6291460
  6.5 330.4 %all-reduce.2.cloned.1.call-start = ((), (), s32[]{:S(2)}) async-start(), calls=%async_computation.2 | async-start | bytes 2097152 | tf_op jit(solution)/shard_map/psum | solution.py:84
  8.2 18.8 %collective-permute-start.1 = (f32[3,16,32,128]{3,2,1,0:T(8,128)S(1)}, f32[3,16,32,128]{3,2,1,0:T(8,128)S(1)}, u32[]{:S(2)}, u32[]{:S(2)}) collective-permute-start(f32[3,16,32,128]{3,2,1,0:T(8,128)S(1)} %get-tuple-element.102), channel_id=1, source_target_pairs={{0,4},{4,8},{8,12},{12,16},{16,20},{20,24},{24,28},{28,0},{1,5},{5... | collective-permute-start | bytes 2359304 | tf_op jit(solution)/shard_map/ppermute | solution.py:22
  8.7 19.8 %collective-permute-start = (f32[3,16,32,128]{3,2,1,0:T(8,128)S(1)}, f32[3,16,32,128]{3,2,1,0:T(8,128)S(1)}, u32[]{:S(2)}, u32[]{:S(2)}) collective-permute-start(f32[3,16,32,128]{3,2,1,0:T(8,128)S(1)} %get-tuple-element.101), channel_id=1, source_target_pairs={{4,0},{8,4},{12,8},{16,12},{20,16},{24,20},{28,24},{0,28},{5,1},{9... | collective-permute-start | bytes 2359304 | tf_op jit(solution)/shard_map/ppermute | solution.py:24
  18.6 3.1 copy-start.2
  43.7 20.8 %collective-permute-start.2 = (f32[3,16,32,128]{3,2,1,0:T(8,128)S(1)}, f32[3,16,32,128]{3,2,1,0:T(8,128)S(1)}, u32[]{:S(2)}, u32[]{:S(2)}) collective-permute-start(f32[3,16,32,128]{3,2,1,0:T(8,128)S(1)} %get-tuple-element.83), channel_id=1, source_target_pairs={{4,0},{8,4},{12,8},{16,12},{20,16},{24,20},{28,24},{0,28},{5,1},{9... | collective-permute-start | bytes 2359304 | tf_op jit(solution)/shard_map/ppermute | solution.py:24
  46.6 18.5 %collective-permute-start.3 = (f32[3,16,32,128]{3,2,1,0:T(8,128)S(1)}, f32[3,16,32,128]{3,2,1,0:T(8,128)S(1)}, u32[]{:S(2)}, u32[]{:S(2)}) collective-permute-start(f32[3,16,32,128]{3,2,1,0:T(8,128)S(1)} %get-tuple-element.84), channel_id=1, source_target_pairs={{0,4},{4,8},{8,12},{12,16},{16,20},{20,24},{24,28},{28,0},{1,5},{5... | collective-permute-start | bytes 2359304 | tf_op jit(solution)/shard_map/ppermute | solution.py:22
  64.5 0.9 copy-start.4
  65.0 1.0 copy-start.7
  84.1 19.5 %collective-permute-start.4 = (f32[3,16,32,128]{3,2,1,0:T(8,128)S(1)}, f32[3,16,32,128]{3,2,1,0:T(8,128)S(1)}, u32[]{:S(2)}, u32[]{:S(2)}) collective-permute-start(f32[3,16,32,128]{3,2,1,0:T(8,128)S(1)} %get-tuple-element.57), channel_id=1, source_target_pairs={{4,0},{8,4},{12,8},{16,12},{20,16},{24,20},{28,24},{0,28},{5,1},{9... | collective-permute-start | bytes 2359304 | tf_op jit(solution)/shard_map/ppermute | solution.py:24
  86.6 17.0 %collective-permute-start.5 = (f32[3,16,32,128]{3,2,1,0:T(8,128)S(1)}, f32[3,16,32,128]{3,2,1,0:T(8,128)S(1)}, u32[]{:S(2)}, u32[]{:S(2)}) collective-permute-start(f32[3,16,32,128]{3,2,1,0:T(8,128)S(1)} %get-tuple-element.58), channel_id=1, source_target_pairs={{0,4},{4,8},{8,12},{12,16},{16,20},{20,24},{24,28},{28,0},{1,5},{5... | collective-permute-start | bytes 2359304 | tf_op jit(solution)/shard_map/ppermute | solution.py:22
  103.6 0.9 copy-start.6
  103.6 1.2 copy-start.9
  122.9 18.6 %collective-permute-start.6 = (f32[3,16,32,128]{3,2,1,0:T(8,128)S(1)}, f32[3,16,32,128]{3,2,1,0:T(8,128)S(1)}, u32[]{:S(2)}, u32[]{:S(2)}) collective-permute-start(f32[3,16,32,128]{3,2,1,0:T(8,128)S(1)} %get-tuple-element.31), channel_id=1, source_target_pairs={{4,0},{8,4},{12,8},{16,12},{20,16},{24,20},{28,24},{0,28},{5,1},{9... | collective-permute-start | bytes 2359304 | tf_op jit(solution)/shard_map/ppermute | solution.py:24
  125.7 16.8 %collective-permute-start.7 = (f32[3,16,32,128]{3,2,1,0:T(8,128)S(1)}, f32[3,16,32,128]{3,2,1,0:T(8,128)S(1)}, u32[]{:S(2)}, u32[]{:S(2)}) collective-permute-start(f32[3,16,32,128]{3,2,1,0:T(8,128)S(1)} %get-tuple-element.32), channel_id=1, source_target_pairs={{0,4},{4,8},{8,12},{12,16},{16,20},{20,24},{24,28},{28,0},{1,5},{5... | collective-permute-start | bytes 2359304 | tf_op jit(solution)/shard_map/ppermute | solution.py:22
  141.5 1.0 copy-start.5
  142.5 0.9 copy-start.8
  339.7 2.9 copy-start.3
  362.3 2.3 copy-start.1
Sparse Core Ops, SparseCore 0:
  206.2 130.6 all-reduce.1

commit v2 on v0

v2 whole, which is shorter than its diff:
```python
import functools

import jax
import jax.numpy as jnp
from jax import lax
from jax.experimental import pallas as pl
from jax.experimental.pallas import tpu as pltpu
from jax.sharding import PartitionSpec as P

DEGREE = 4
NS_ITERS = 8

STENCIL_WEIGHTS = [-49.0 / 18.0, 3.0 / 2.0, -3.0 / 20.0, 1.0 / 90.0]
CENTER = 5.0
HALF_WIDTH = 4.0
REACH = 3
CHUNKS = 4
MESH = pl.DeviceIdType.MESH


def split(value):
    high = value.astype(jnp.bfloat16)
    low = (value - high.astype(jnp.float32)).astype(jnp.bfloat16)
    return high, low


def product(left, right):
    def dot(a, b):
        return jnp.dot(a, b, preferred_element_type=jnp.float32)

    return dot(left[0], right[0]) + (dot(left[0], right[1]) + dot(left[1], right[0]))


def transposed_dot(left, right):
    return lax.dot_general(
        left, right, (((0,), (0,)), ((), ())), preferred_element_type=jnp.float32
    )


def kernel(
    n_space, n_orb, x_ref, coef_ref, out_ref,
    fields, last, mixed, high, low, part, cross, landed, summed, landed_cols, total, y_ref, z_ref, white,
    load_sem, halo_send, halo_recv, to_send, to_recv, to_own,
    rows_send, rows_recv, cols_send, cols_recv, gcols_send, gcols_recv, grows_send, grows_recv,
    back_send, back_recv, back_own,
):
    planes, ny, nz, lanes = x_ref.shape
    norb = total.shape[0]
    rows = ny // CHUNKS
    share = planes // n_orb
    cells = share * rows * nz
    piece = norb // n_space
    me_s = lax.axis_index("space")
    me_o = lax.axis_index("orb")
    left = lax.rem(me_s + n_space - 1, n_space)
    right = lax.rem(me_s + 1, n_space)

    def space_peer(offset):
        return lax.rem(me_s + offset, n_space)

    def orb_peer(offset):
        return lax.rem(me_o + offset, n_orb)

    def row_block(device):
        return pl.ds(pl.multiple_of(device * piece, piece), piece)

    def lane_block(device):
        return pl.ds(pl.multiple_of(device * lanes, lanes), lanes)

    def remote(src, dst, send, recv, space, orb):
        return pltpu.make_async_remote_copy(
            src_ref=src, dst_ref=dst, send_sem=send, recv_sem=recv,
            device_id=(space, orb), device_id_type=MESH,
        )

    load = pltpu.make_async_copy(x_ref, fields.at[0, pl.ds(REACH, planes)], load_sem)
    load.start()

    barrier = pltpu.get_barrier_semaphore()
    for offset in range(1, n_space):
        pl.semaphore_signal(barrier, inc=1, device_id=(space_peer(offset), me_o), device_id_type=MESH)
    for offset in range(1, n_orb):
        pl.semaphore_signal(barrier, inc=1, device_id=(me_s, orb_peer(offset)), device_id_type=MESH)
    pl.semaphore_wait(barrier, n_space + n_orb - 2)

    def halo(step, chunk, side):
        start, landing = ((REACH, REACH + planes), (planes, 0))[side]
        ys = pl.ds(chunk * rows, rows)
        return remote(
            fields.at[step, pl.ds(start, REACH), ys],
            fields.at[step, pl.ds(landing, REACH), ys],
            halo_send.at[step, chunk, side],
            halo_recv.at[step, chunk, side],
            (left, right)[side],
            me_o,
        )

    def outward(chunk, offset):
        peer = orb_peer(offset)
        return remote(
            last.at[pl.ds(peer * share, share), pl.ds(chunk * rows, rows)],
            mixed.at[chunk, :, :, :, lane_block(me_o)],
            to_send.at[chunk, offset],
            to_recv.at[chunk, offset],
            me_s,
            peer,
        )

    def outward_own(chunk):
        return pltpu.make_async_copy(
            last.at[pl.ds(me_o * share, share), pl.ds(chunk * rows, rows)],
            mixed.at[chunk, :, :, :, lane_block(me_o)],
            to_own.at[chunk],
        )

    def back(chunk, offset):
        peer = orb_peer(offset)
        return remote(
            white.at[chunk, :, :, :, lane_block(peer)],
            out_ref.at[pl.ds(me_o * share, share), pl.ds(chunk * rows, rows)],
            back_send.at[chunk, offset],
            back_recv.at[chunk, offset],
            me_s,
            peer,
        )

    def back_own_copy(chunk):
        return pltpu.make_async_copy(
            white.at[chunk, :, :, :, lane_block(me_o)],
            out_ref.at[pl.ds(me_o * share, share), pl.ds(chunk * rows, rows)],
            back_own.at[chunk],
        )

    load.wait()

    @pl.loop(0, CHUNKS)
    def _(chunk):
        halo(0, chunk, 0).start()
        halo(0, chunk, 1).start()

    for step in range(DEGREE):
        scale = (1.0 if step == 0 else 2.0) / HALF_WIDTH
        weights = [-0.5 * scale * w for w in STENCIL_WEIGHTS]

        @pl.loop(0, CHUNKS)
        def _(chunk):
            halo(step, chunk, 0).wait_recv()
            halo(step, chunk, 1).wait_recv()

            @pl.loop(0, planes)
            def _(plane):
                for row in range(rows):
                    y = chunk * rows + row
                    here = fields[step, plane + REACH, y]
                    value = (scale * coef_ref[plane, y]) * here
                    for k in range(1, REACH + 1):
                        along = (
                            fields[step, plane + (REACH + k), y] + fields[step, plane + (REACH - k), y]
                        ) + (
                            fields[step, plane + REACH, lax.rem(y + k, ny)]
                            + fields[step, plane + REACH, lax.rem(y + (ny - k), ny)]
                        )
                        along = along + (pltpu.roll(here, k, 0) + pltpu.roll(here, nz - k, 0))
                        value = value + weights[k] * along
                    if step > 0:
                        value = value - fields[step - 1, plane + REACH, y]
                    if step < DEGREE - 1:
                        fields[step + 1, plane + REACH, y] = value
                    else:
                        last[plane, y] = value

            if step < DEGREE - 1:
                halo(step + 1, chunk, 0).start()
                halo(step + 1, chunk, 1).start()
            else:
                for offset in range(1, n_orb):
                    outward(chunk, offset).start()
                outward_own(chunk).start()

    part[...] = jnp.zeros_like(part)
    cross[...] = jnp.zeros_like(cross)

    @pl.loop(0, CHUNKS)
    def _(chunk):
        for offset in range(1, n_orb):
            outward(chunk, offset).wait_recv()
        outward_own(chunk).wait()
        head, tail = split(mixed[chunk].reshape(cells, norb))
        at = pl.ds(pl.multiple_of(chunk * cells, cells), cells)
        high[at] = head
        low[at] = tail
        part[...] += transposed_dot(head, head)
        cross[...] += transposed_dot(head, tail)

    part[...] = (part[...] + 2.0 * cross[...]) * (1.0 / (CHUNKS * cells * n_space * n_orb))

    def send_rows(offset):
        peer = space_peer(offset)
        return remote(
            part.at[row_block(peer)], landed.at[offset - 1],
            rows_send.at[offset], rows_recv.at[offset], peer, me_o,
        )

    def send_cols(offset):
        peer = orb_peer(offset)
        return remote(
            summed.at[:, lane_block(peer)], landed_cols.at[offset - 1],
            cols_send.at[offset], cols_recv.at[offset], me_s, peer,
        )

    def gather_cols(offset):
        block = total.at[row_block(me_s), lane_block(me_o)]
        return remote(block, block, gcols_send.at[offset], gcols_recv.at[offset], me_s, orb_peer(offset))

    def gather_rows(offset):
        block = total.at[row_block(me_s)]
        return remote(block, block, grows_send.at[offset], grows_recv.at[offset], space_peer(offset), me_o)

    for offset in range(1, n_space):
        send_rows(offset).start()
    value = part[row_block(me_s)]
    for offset in range(1, n_space):
        send_rows(offset).wait_recv()
        value = value + landed[offset - 1]
    summed[...] = value
    for offset in range(1, n_orb):
        send_cols(offset).start()
    value = summed[:, lane_block(me_o)]
    for offset in range(1, n_orb):
        send_cols(offset).wait_recv()
        value = value + landed_cols[offset - 1]
    total[row_block(me_s), lane_block(me_o)] = value
    for offset in range(1, n_orb):
        gather_cols(offset).start()
    for offset in range(1, n_orb):
        gather_cols(offset).wait_recv()
    for offset in range(1, n_space):
        gather_rows(offset).start()
    for offset in range(1, n_space):
        gather_rows(offset).wait_recv()

    one_sided = total[...]
    intersection = 0.5 * (one_sided + one_sided.T)
    squares = jnp.sum(intersection * intersection, axis=0, keepdims=True)
    norm_scale = jnp.sqrt(jnp.sum(squares, axis=1, keepdims=True) + 1e-06)
    on_diagonal = lax.broadcasted_iota(jnp.int32, (norb, norb), 0) == lax.broadcasted_iota(
        jnp.int32, (norb, norb), 1
    )

    def factor_of(term):
        return jnp.where(on_diagonal, 1.5, 0.0) - 0.5 * term

    scaled = intersection / norm_scale
    inverse = factor_of(scaled)
    z_ref[...] = inverse
    y_ref[...] = product(split(scaled), split(inverse))

    @pl.loop(1, NS_ITERS - 1)
    def _(step):
        ys, zs = split(y_ref[...]), split(z_ref[...])
        fs = split(factor_of(product(zs, ys)))
        y_ref[...] = product(ys, fs)
        z_ref[...] = product(fs, zs)

    ys, zs = split(y_ref[...]), split(z_ref[...])
    fs = split(factor_of(product(zs, ys)))
    z_ref[...] = product(fs, zs) / jnp.sqrt(norm_scale)

    @pl.loop(0, CHUNKS)
    def _(chunk):
        at = pl.ds(pl.multiple_of(chunk * cells, cells), cells)
        value = product((high[at], low[at]), split(z_ref[...]))
        white[chunk] = value.reshape(share, rows, nz, norb)
        for offset in range(1, n_orb):
            back(chunk, offset).start()
        back_own_copy(chunk).start()

    for offset in range(1, n_space):
        send_rows(offset).wait_send()
        gather_rows(offset).wait_send()
    for offset in range(1, n_orb):
        send_cols(offset).wait_send()
        gather_cols(offset).wait_send()
    for step in range(DEGREE):

        @pl.loop(0, CHUNKS)
        def _(chunk):
            halo(step, chunk, 0).wait_send()
            halo(step, chunk, 1).wait_send()

    @pl.loop(0, CHUNKS)
    def _(chunk):
        back_own_copy(chunk).wait()
        for offset in range(1, n_orb):
            outward(chunk, offset).wait_send()
            back(chunk, offset).wait()


def body(n_space, n_orb, orbitals, potential):
    planes, ny, nz, lanes = orbitals.shape
    norb = lanes * n_orb
    piece = norb // n_space
    block = (CHUNKS, planes // n_orb, ny // CHUNKS, nz, norb)
    cells = planes * ny * nz // n_orb
    coef = potential - (CENTER + 1.5 * STENCIL_WEIGHTS[0])
    coef = jnp.broadcast_to(coef[..., None], orbitals.shape)
    f32 = jnp.float32
    dma = pltpu.SemaphoreType.DMA
    return pl.pallas_call(
        functools.partial(kernel, n_space, n_orb),
        out_shape=jax.ShapeDtypeStruct(orbitals.shape, f32),
        in_specs=[pl.BlockSpec(memory_space=pl.ANY), pl.BlockSpec(memory_space=pltpu.VMEM)],
        out_specs=pl.BlockSpec(memory_space=pltpu.VMEM),
        scratch_shapes=[
            pltpu.VMEM((DEGREE, planes + 2 * REACH, ny, nz, lanes), f32),
            pltpu.VMEM((planes, ny, nz, lanes), f32),
            pltpu.VMEM(block, f32),
            pltpu.VMEM((cells, norb), jnp.bfloat16),
            pltpu.VMEM((cells, norb), jnp.bfloat16),
            pltpu.VMEM((norb, norb), f32),
            pltpu.VMEM((norb, norb), f32),
            pltpu.VMEM((n_space - 1, piece, norb), f32),
            pltpu.VMEM((piece, norb), f32),
            pltpu.VMEM((n_orb - 1, piece, lanes), f32),
            pltpu.VMEM((norb, norb), f32),
            pltpu.VMEM((norb, norb), f32),
            pltpu.VMEM((norb, norb), f32),
            pltpu.VMEM(block, f32),
            dma,
            dma((DEGREE, CHUNKS, 2)),
            dma((DEGREE, CHUNKS, 2)),
            dma((CHUNKS, n_orb)),
            dma((CHUNKS, n_orb)),
            dma((CHUNKS,)),
            dma((n_space,)),
            dma((n_space,)),
            dma((n_orb,)),
            dma((n_orb,)),
            dma((n_orb,)),
            dma((n_orb,)),
            dma((n_space,)),
            dma((n_space,)),
            dma((CHUNKS, n_orb)),
            dma((CHUNKS, n_orb)),
            dma((CHUNKS,)),
        ],
        compiler_params=pltpu.CompilerParams(
            collective_id=0, has_side_effects=True, vmem_limit_bytes=60 * 1024 * 1024
        ),
        cost_estimate=pl.CostEstimate(
            flops=20_000_000_000, bytes_accessed=8_000_000, transcendentals=0
        ),
    )(orbitals, coef)


def solution(mesh):
    return jax.shard_map(
        functools.partial(body, mesh.shape["space"], mesh.shape["orb"]),
        mesh=mesh,
        in_specs=(P("space", None, None, "orb"), P("space", None, None)),
        out_specs=P("space", None, None, "orb"),
        check_vma=False,
    )
```

time: 448 us -> 217 us (0.48); the launches traced: 440 us -> 216 us
  waiting for transfers between devices: 258 us -> 0 us
  Pallas kernels: 0 us -> 211 us
  matrix products: 71.6 us -> 0 us
  local copies, waits for them, and re-layouts: 44.7 us -> 5 us
  other arithmetic: 38.2 us -> 0.85 us
  between operations: 15.1 us -> 0.01 us
  starting transfers between devices: 11.9 us -> 0 us
    pallas_call x0 -> x1, Pallas kernels: none -> 211 us  [body(): pl.pallas_call(functools.partial(kernel, n_space, n_orb), out_shape=jax.S...]
    all_gather x1 -> x0, waiting for transfers between devices: 151 us -> none  [body(): gathered = lax.all_gather(cell_rows, 'orb', axis=1, tiled=True)]
    dot_general x25 -> x0, matrix products: 71.6 us -> none  [the longest x1 18.7 us: body(): jnp.dot(gathered.T, gathered, precision=lax.Precision.HIGHEST)]
    psum x1 -> x0, waiting for transfers between devices: 54.9 us -> none  [body(): intersection = lax.psum(partial_terms, 'space') / total_cells]
    ppermute x8 -> x0, waiting for transfers between devices: 52.4 us -> none  [the longest x4 46.1 us: padded_2(): lax.ppermute(head, axis, [((i + 1) % count, i) for i in range(count)])]
    slice x52 -> x0, local copies, waits for them, and re-layouts: 40.8 us -> none  [the longest x24 25.3 us: slab_hamiltonian(): along_second = jnp.roll(field, offset, 1) + jnp.roll(field, -offset, 1)]
    sub x3 -> x1, other arithmetic: 28.8 us -> 0.85 us  [body(): coef = potential - (CENTER + 1.5 * STENCIL_WEIGHTS[0])]
    ppermute x8 -> x0, starting transfers between devices: 11.8 us -> none  [the longest x4 11.1 us: padded_2(): lax.ppermute(head, axis, [((i + 1) % count, i) for i in range(count)])]
  transfers between devices with their start and end apart: 10 -> 0, of which waited for: 9 -> 0; matrix products, arithmetic and copies ran while one was open for 4% -> 0% of each run, Pallas kernels for 0% -> 0%
where the time goes in v2:
time: 217 us; the launch traced here: 216 us
  Pallas kernels  211 us (97%)
  local copies, waits for them, and re-layouts  5 us (2%)
    pallas_call x1, Pallas kernels, body(): pl.pallas_call(functools.partial(kernel, n_space, n_orb), out_shape=jax.S...  211 us

profile of v2, /device:TPU:0, one launch (start us, length us, event | category | flops | bytes accessed | tf_op | source)
XLA Modules:
  0.0 216.5 jit_solution(4344587860093722575)
XLA Ops:
  0.0 0.8 broadcast_add_fusion
  0.8 1.9 broadcast_in_dim.2.coef_ref
  2.8 210.6 %shard_map.28 = f32[8,16,32,128]{3,2,1,0:T(8,128)} custom-call(f32[8,16,32,128]{3,2,1,0:T(8,128)} %x_ref.1, f32[8,16,32,128]{3,2,1,0:T(8,128)} %broadcast_in_dim.2.coef_ref), custom_call_target="tpu_custom_call" | custom-call | flops 20000000000 | bytes 8000000 | tf_op jit(solution)/shard_map/pallas_call | solution.py:309
  213.4 3.1 %copy.4 = f32[8,16,32,128]{3,2,1,0:T(8,128)} copy(f32[8,16,32,128]{3,2,1,0:T(8,128)} %shard_map.28) | data formatting | bytes 4194304

commit v3 on v2

--- a/solution.py
+++ b/solution.py
@@ -39,7 +39,7 @@
 
 def kernel(
     n_space, n_orb, x_ref, coef_ref, out_ref,
-    fields, last, mixed, high, low, part, cross, landed, summed, landed_cols, total, y_ref, z_ref, white,
+    raw, fields, last, mixed, high, low, part, cross, landed, summed, landed_cols, total, y_ref, z_ref, white,
     load_sem, halo_send, halo_recv, to_send, to_recv, to_own,
     rows_send, rows_recv, cols_send, cols_recv, gcols_send, gcols_recv, grows_send, grows_recv,
     back_send, back_recv, back_own,
@@ -49,6 +49,8 @@
     rows = ny // CHUNKS
     share = planes // n_orb
     cells = share * rows * nz
+    deep = nz // 2
+    turn = lanes // 2
     piece = norb // n_space
     me_s = lax.axis_index("space")
     me_o = lax.axis_index("orb")
@@ -73,7 +75,7 @@
             device_id=(space, orb), device_id_type=MESH,
         )
 
-    load = pltpu.make_async_copy(x_ref, fields.at[0, pl.ds(REACH, planes)], load_sem)
+    load = pltpu.make_async_copy(x_ref, raw, load_sem)
     load.start()
 
     barrier = pltpu.get_barrier_semaphore()
@@ -83,34 +85,34 @@
         pl.semaphore_signal(barrier, inc=1, device_id=(me_s, orb_peer(offset)), device_id_type=MESH)
     pl.semaphore_wait(barrier, n_space + n_orb - 2)
 
-    def halo(step, chunk, side):
+    def halo(half, step, chunk, side):
         start, landing = ((REACH, REACH + planes), (planes, 0))[side]
         ys = pl.ds(chunk * rows, rows)
         return remote(
-            fields.at[step, pl.ds(start, REACH), ys],
-            fields.at[step, pl.ds(landing, REACH), ys],
-            halo_send.at[step, chunk, side],
-            halo_recv.at[step, chunk, side],
+            fields.at[half, step, pl.ds(start, REACH), ys],
+            fields.at[half, step, pl.ds(landing, REACH), ys],
+            halo_send.at[half, step, chunk, side],
+            halo_recv.at[half, step, chunk, side],
             (left, right)[side],
             me_o,
         )
 
-    def outward(chunk, offset):
+    def outward(half, chunk, offset):
         peer = orb_peer(offset)
         return remote(
-            last.at[pl.ds(peer * share, share), pl.ds(chunk * rows, rows)],
-            mixed.at[chunk, :, :, :, lane_block(me_o)],
-            to_send.at[chunk, offset],
-            to_recv.at[chunk, offset],
+            last.at[half, pl.ds(peer * share, share), pl.ds(chunk * rows, rows)],
+            mixed.at[half, chunk, :, :, :, lane_block(me_o)],
+            to_send.at[half, chunk, offset],
+            to_recv.at[half, chunk, offset],
             me_s,
             peer,
         )
 
-    def outward_own(chunk):
+    def outward_own(half, chunk):
         return pltpu.make_async_copy(
-            last.at[pl.ds(me_o * share, share), pl.ds(chunk * rows, rows)],
-            mixed.at[chunk, :, :, :, lane_block(me_o)],
-            to_own.at[chunk],
+            last.at[half, pl.ds(me_o * share, share), pl.ds(chunk * rows, rows)],
+            mixed.at[half, chunk, :, :, :, lane_block(me_o)],
+            to_own.at[half, chunk],
         )
 
     def back(chunk, offset):
@@ -132,63 +134,115 @@
         )
 
     load.wait()
+    first_lanes = lax.broadcasted_iota(jnp.int32, (deep, lanes), 1) < turn
+    sublane = lax.broadcasted_iota(jnp.int32, (8, lanes), 0)
+
+    def turned(value):
+        return pltpu.roll(value, turn, value.ndim - 1)
+
+    @pl.loop(0, planes)
+    def _(plane):
+        @pl.loop(0, ny)
+        def _(y):
+            top, bottom = raw[plane, y, :deep], raw[plane, y, deep:]
+            fields[0, 0, plane + REACH, y] = jnp.where(first_lanes, top, turned(bottom))
+            fields[1, 0, plane + REACH, y] = jnp.where(first_lanes, turned(top), bottom)
+
+    def send_halos(half, step):
+        @pl.loop(0, CHUNKS)
+        def _(chunk):
+            halo(half, step, chunk, 0).start()
+            halo(half, step, chunk, 1).start()
+
+    def along_depth(here):
+        other = turned(here)
+        inner = [here[i : i + 8] for i in range(0, deep, 8)]
+        groups = [other[deep - 8 :]] + inner + [other[:8]]
+        sums = []
+        for k in range(1, REACH + 1):
+            up = [pltpu.roll(group, k, 0) for group in groups[:-1]]
+            down = [pltpu.roll(group, 8 - k, 0) for group in groups[1:]]
+            sums.append(
+                jnp.concatenate(
+                    [
+                        jnp.where(sublane < k, up[i], up[i + 1])
+                        + jnp.where(sublane >= 8 - k, down[i + 1], down[i])
+                        for i in range(len(inner))
+                    ],
+                    axis=0,
+                )
+            )
+        return sums
+
+    def filter_step(half, step):
+        scale = (1.0 if step == 0 else 2.0) / HALF_WIDTH
+        weights = [-0.5 * scale * w for w in STENCIL_WEIGHTS]
+
+        @pl.loop(0, CHUNKS)
+        def _(chunk):
+            halo(half, step, chunk, 0).wait_recv()
+            halo(half, step, chunk, 1).wait_recv()
+
+            @pl.loop(0, planes)
+            def _(plane):
+                at = plane + REACH
+                for row in range(rows):
+                    y = chunk * rows + row
+                    here = fields[half, step, at, y]
+                    value = (scale * coef_ref[plane, y]) * here
+                    depth = along_depth(here)
+                    for k in range(1, REACH + 1):
+                        along = (fields[half, step, at + k, y] + fields[half, step, at - k, y]) + (
+                            fields[half, step, at, lax.rem(y + k, ny)]
+                            + fields[half, step, at, lax.rem(y + (ny - k), ny)]
+                        )
+                        value = value + weights[k] * (along + depth[k - 1])
+                    if step > 0:
+                        value = value - fields[half, step - 1, at, y]
+                    if step < DEGREE - 1:
+                        fields[half, step + 1, at, y] = value
+                    else:
+                        last[half, plane, y] = value
+
+            if step < DEGREE - 1:
+                halo(half, step + 1, chunk, 0).start()
+                halo(half, step + 1, chunk, 1).start()
+            else:
+                for offset in range(1, n_orb):
+                    outward(half, chunk, offset).start()
+                outward_own(half, chunk).start()
+
+    send_halos(0, 0)
+    for step in range(DEGREE - 2):
+        filter_step(0, step)
+    send_halos(1, 0)
+    filter_step(0, DEGREE - 2)
+    filter_step(1, 0)
+    filter_step(0, DEGREE - 1)
+    for step in range(1, DEGREE):
+        filter_step(1, step)
+
+    part[...] = jnp.zeros_like(part)
+    cross[...] = jnp.zeros_like(cross)
 
     @pl.loop(0, CHUNKS)
     def _(chunk):
-        halo(0, chunk, 0).start()
-        halo(0, chunk, 1).start()
-
-    for step in range(DEGREE):
-        scale = (1.0 if step == 0 else 2.0) / HALF_WIDTH
-        weights = [-0.5 * scale * w for w in STENCIL_WEIGHTS]
-
-        @pl.loop(0, CHUNKS)
-        def _(chunk):
-            halo(step, chunk, 0).wait_recv()
-            halo(step, chunk, 1).wait_recv()
-
-            @pl.loop(0, planes)
-            def _(plane):
-                for row in range(rows):
-                    y = chunk * rows + row
-                    here = fields[step, plane + REACH, y]
-                    value = (scale * coef_ref[plane, y]) * here
-                    for k in range(1, REACH + 1):
-                        along = (
-                            fields[step, plane + (REACH + k), y] + fields[step, plane + (REACH - k), y]
-                        ) + (
-                            fields[step, plane + REACH, lax.rem(y + k, ny)]
-                            + fields[step, plane + REACH, lax.rem(y + (ny - k), ny)]
-                        )
-                        along = along + (pltpu.roll(here, k, 0) + pltpu.roll(here, nz - k, 0))
-                        value = value + weights[k] * along
-                    if step > 0:
-                        value = value - fields[step - 1, plane + REACH, y]
-                    if step < DEGREE - 1:
-                        fields[step + 1, plane + REACH, y] = value
-                    else:
-                        last[plane, y] = value
-
-            if step < DEGREE - 1:
-                halo(step + 1, chunk, 0).start()
-                halo(step + 1, chunk, 1).start()
-            else:
-                for offset in range(1, n_orb):
-                    outward(chunk, offset).start()
-                outward_own(chunk).start()
-
-    part[...] = jnp.zeros_like(part)
-    cross[...] = jnp.zeros_like(cross)
-
-    @pl.loop(0, CHUNKS)
-    def _(chunk):
-        for offset in range(1, n_orb):
-            outward(chunk, offset).wait_recv()
-        outward_own(chunk).wait()
-        head, tail = split(mixed[chunk].reshape(cells, norb))
         at = pl.ds(pl.multiple_of(chunk * cells, cells), cells)
-        high[at] = head
-        low[at] = tail
+        for half in range(2):
+            for offset in range(1, n_orb):
+                outward(half, chunk, offset).wait_recv()
+            outward_own(half, chunk).wait()
+        for block in range(n_orb):
+            columns = pl.ds(block * lanes, lanes)
+            shape = (share * rows, deep, lanes)
+            one = mixed[0, chunk, :, :, :, columns].reshape(shape)
+            two = mixed[1, chunk, :, :, :, columns].reshape(shape)
+            lower = lax.broadcasted_iota(jnp.int32, shape, 2) < turn
+            whole = jnp.concatenate(
+                [jnp.where(lower, one, turned(two)), jnp.where(lower, turned(one), two)], axis=1
+            )
+            high[at, columns], low[at, columns] = split(whole.reshape(cells, lanes))
+        head, tail = high[at], low[at]
         part[...] += transposed_dot(head, head)
         cross[...] += transposed_dot(head, tail)
 
@@ -281,18 +335,20 @@
     for offset in range(1, n_orb):
         send_cols(offset).wait_send()
         gather_cols(offset).wait_send()
-    for step in range(DEGREE):
-
-        @pl.loop(0, CHUNKS)
-        def _(chunk):
-            halo(step, chunk, 0).wait_send()
-            halo(step, chunk, 1).wait_send()
+    for half in range(2):
+        for step in range(DEGREE):
+
+            @pl.loop(0, CHUNKS)
+            def _(chunk):
+                halo(half, step, chunk, 0).wait_send()
+                halo(half, step, chunk, 1).wait_send()
 
     @pl.loop(0, CHUNKS)
     def _(chunk):
         back_own_copy(chunk).wait()
         for offset in range(1, n_orb):
-            outward(chunk, offset).wait_send()
+            outward(0, chunk, offset).wait_send()
+            outward(1, chunk, offset).wait_send()
             back(chunk, offset).wait()
 
 
@@ -303,7 +359,9 @@
     block = (CHUNKS, planes // n_orb, ny // CHUNKS, nz, norb)
     cells = planes * ny * nz // n_orb
     coef = potential - (CENTER + 1.5 * STENCIL_WEIGHTS[0])
-    coef = jnp.broadcast_to(coef[..., None], orbitals.shape)
+    coef = jnp.swapaxes(coef.reshape(planes, ny, 2, nz // 2), 2, 3)
+    coef = jnp.broadcast_to(coef[..., None], coef.shape + (lanes // 2,))
+    coef = coef.reshape(planes, ny, nz // 2, lanes)
     f32 = jnp.float32
     dma = pltpu.SemaphoreType.DMA
     return pl.pallas_call(
@@ -312,9 +370,10 @@
         in_specs=[pl.BlockSpec(memory_space=pl.ANY), pl.BlockSpec(memory_space=pltpu.VMEM)],
         out_specs=pl.BlockSpec(memory_space=pltpu.VMEM),
         scratch_shapes=[
-            pltpu.VMEM((DEGREE, planes + 2 * REACH, ny, nz, lanes), f32),
             pltpu.VMEM((planes, ny, nz, lanes), f32),
-            pltpu.VMEM(block, f32),
+            pltpu.VMEM((2, DEGREE, planes + 2 * REACH, ny, nz // 2, lanes), f32),
+            pltpu.VMEM((2, planes, ny, nz // 2, lanes), f32),
+            pltpu.VMEM((2,) + block[:3] + (nz // 2, norb), f32),
             pltpu.VMEM((cells, norb), jnp.bfloat16),
             pltpu.VMEM((cells, norb), jnp.bfloat16),
             pltpu.VMEM((norb, norb), f32),
@@ -327,11 +386,11 @@
             pltpu.VMEM((norb, norb), f32),
             pltpu.VMEM(block, f32),
             dma,
-            dma((DEGREE, CHUNKS, 2)),
-            dma((DEGREE, CHUNKS, 2)),
-            dma((CHUNKS, n_orb)),
-            dma((CHUNKS, n_orb)),
-            dma((CHUNKS,)),
+            dma((2, DEGREE, CHUNKS, 2)),
+            dma((2, DEGREE, CHUNKS, 2)),
+            dma((2, CHUNKS, n_orb)),
+            dma((2, CHUNKS, n_orb)),
+            dma((2, CHUNKS)),
             dma((n_space,)),
             dma((n_space,)),
             dma((n_orb,)),

time: 217 us -> 214 us (0.986)
  Pallas kernels: 211 us -> 203 us
  local copies, waits for them, and re-layouts: 5 us -> 8.59 us
    pallas_call x1, Pallas kernels: 211 us -> 203 us  [body(): pl.pallas_call(functools.partial(kernel, n_space, n_orb), out_shape=jax.S...]
    reshape x0 -> x2, local copies, waits for them, and re-layouts: none -> 2.26 us  [the longest x1 2.13 us: body(): coef = coef.reshape(planes, ny, nz // 2, lanes)]
where the time goes in v3:
time: 214 us; the launch traced here: 213 us
  Pallas kernels  203 us (95%)
  local copies, waits for them, and re-layouts  8.59 us (4%)
    pallas_call x1, Pallas kernels, body(): pl.pallas_call(functools.partial(kernel, n_space, n_orb), out_shape=jax.S...  203 us

profile of v3, /device:TPU:0, one launch (start us, length us, event | category | flops | bytes accessed | tf_op | source)
XLA Modules:
  0.0 212.7 jit_solution(14122081307396448927)
XLA Ops:
  0.0 0.8 broadcast_add_fusion
  0.8 0.1 reshape.7
  1.0 0.8 copy.3
  1.8 2.4 %broadcast_in_dim.2 = f32[8,16,16,2,64]{4,3,2,1,0:T(2,128)S(1)} broadcast(f32[8,16,16,2]{3,2,1,0:T(8,128)S(1)} %copy.3), dimensions={0,1,2,3} | broadcast | bytes 1064960 | tf_op jit(solution)/shard_map/broadcast_in_dim | solution.py:363
  4.2 2.1 %reshape.8.coef_ref = f32[8,16,16,128]{3,2,1,0:T(8,128)} reshape(f32[8,16,16,2,64]{4,3,2,1,0:T(2,128)S(1)} %broadcast_in_dim.2) | data formatting | bytes 2097152 | tf_op jit(solution)/shard_map/reshape | solution.py:364
  6.4 203.2 %shard_map.28 = f32[8,16,32,128]{3,2,1,0:T(8,128)} custom-call(f32[8,16,32,128]{3,2,1,0:T(8,128)} %x_ref.1, f32[8,16,16,128]{3,2,1,0:T(8,128)} %reshape.8.coef_ref), custom_call_target="tpu_custom_call" | custom-call | flops 20000000000 | bytes 8000000 | tf_op jit(solution)/shard_map/pallas_call | solution.py:367
  209.6 3.1 %copy.5 = f32[8,16,32,128]{3,2,1,0:T(8,128)} copy(f32[8,16,32,128]{3,2,1,0:T(8,128)} %shard_map.28) | data formatting | bytes 4194304

commit v4 on v3

--- a/solution.py
+++ b/solution.py
@@ -15,6 +15,7 @@
 HALF_WIDTH = 4.0
 REACH = 3
 CHUNKS = 4
+GATHERED = 2
 MESH = pl.DeviceIdType.MESH
 
 
@@ -25,10 +26,11 @@
 
 
 def product(left, right):
-    def dot(a, b):
-        return jnp.dot(a, b, preferred_element_type=jnp.float32)
-
-    return dot(left[0], right[0]) + (dot(left[0], right[1]) + dot(left[1], right[0]))
+    return jnp.dot(
+        jnp.concatenate([left[0], left[0], left[1]], axis=1),
+        jnp.concatenate([right[0], right[1], right[0]], axis=0),
+        preferred_element_type=jnp.float32,
+    )
 
 
 def transposed_dot(left, right):
@@ -38,9 +40,9 @@
 
 
 def kernel(
-    n_space, n_orb, x_ref, coef_ref, out_ref,
-    raw, fields, last, mixed, high, low, part, cross, landed, summed, landed_cols, total, y_ref, z_ref, white,
-    load_sem, halo_send, halo_recv, to_send, to_recv, to_own,
+    n_space, n_orb, x_ref, potential_ref, out_ref,
+    raw, coef_ref, fields, last, mixed, extra, high, low, part, cross, landed, summed, landed_cols, total, y_ref, z_ref, white,
+    load_sem, halo_send, halo_recv, to_send, to_recv, to_own, extra_send, extra_recv,
     rows_send, rows_recv, cols_send, cols_recv, gcols_send, gcols_recv, grows_send, grows_recv,
     back_send, back_recv, back_own,
 ):
@@ -115,10 +117,27 @@
             to_own.at[half, chunk],
         )
 
+    def gather(half, chunk, offset, turn_at):
+        peer = orb_peer(offset)
+        owner = lax.rem(peer + turn_at, n_orb)
+        return remote(
+            last.at[half, pl.ds(owner * share, share), pl.ds(chunk * rows, rows)],
+            extra.at[half, chunk, turn_at, :, :, :, lane_block(me_o)],
+            extra_send.at[half, chunk, offset, turn_at],
+            extra_recv.at[half, chunk, offset, turn_at],
+            me_s,
+            peer,
+        )
+
+    def gather_start(half, chunk):
+        for turn_at in range(1, n_orb):
+            for offset in range(1, n_orb):
+                gather(half, chunk, offset, turn_at).start()
+
     def back(chunk, offset):
         peer = orb_peer(offset)
         return remote(
-            white.at[chunk, :, :, :, lane_block(peer)],
+            white.at[chunk - GATHERED, :, :, :, lane_block(peer)],
             out_ref.at[pl.ds(me_o * share, share), pl.ds(chunk * rows, rows)],
             back_send.at[chunk, offset],
             back_recv.at[chunk, offset],
@@ -128,7 +147,7 @@
 
     def back_own_copy(chunk):
         return pltpu.make_async_copy(
-            white.at[chunk, :, :, :, lane_block(me_o)],
+            white.at[chunk - GATHERED, :, :, :, lane_block(me_o)],
             out_ref.at[pl.ds(me_o * share, share), pl.ds(chunk * rows, rows)],
             back_own.at[chunk],
         )
@@ -213,6 +232,15 @@
                 outward_own(half, chunk).start()
 
     send_halos(0, 0)
+
+    @pl.loop(0, planes)
+    def _(plane):
+        levels = potential_ref[plane] - (CENTER + 1.5 * STENCIL_WEIGHTS[0])
+        for y in range(ny):
+            front = jnp.broadcast_to(levels[:, y : y + 1], (deep, lanes))
+            rear = jnp.broadcast_to(levels[:, ny + y : ny + y + 1], (deep, lanes))
+            coef_ref[plane, y] = jnp.where(first_lanes, front, rear)
+
     for step in range(DEGREE - 2):
         filter_step(0, step)
     send_halos(1, 0)
@@ -221,6 +249,17 @@
     filter_step(0, DEGREE - 1)
     for step in range(1, DEGREE):
         filter_step(1, step)
+
+    gather_start(0, 0)
+
+    def unpacked(one, two):
+        shape = (share * rows, deep, lanes)
+        one, two = one.reshape(shape), two.reshape(shape)
+        lower = lax.broadcasted_iota(jnp.int32, shape, 2) < turn
+        whole = jnp.concatenate(
+            [jnp.where(lower, one, turned(two)), jnp.where(lower, turned(one), two)], axis=1
+        )
+        return split(whole.reshape(cells, lanes))
 
     part[...] = jnp.zeros_like(part)
     cross[...] = jnp.zeros_like(cross)
@@ -234,14 +273,9 @@
             outward_own(half, chunk).wait()
         for block in range(n_orb):
             columns = pl.ds(block * lanes, lanes)
-            shape = (share * rows, deep, lanes)
-            one = mixed[0, chunk, :, :, :, columns].reshape(shape)
-            two = mixed[1, chunk, :, :, :, columns].reshape(shape)
-            lower = lax.broadcasted_iota(jnp.int32, shape, 2) < turn
-            whole = jnp.concatenate(
-                [jnp.where(lower, one, turned(two)), jnp.where(lower, turned(one), two)], axis=1
+            high[at, columns], low[at, columns] = unpacked(
+                mixed[0, chunk, :, :, :, columns], mixed[1, chunk, :, :, :, columns]
             )
-            high[at, columns], low[at, columns] = split(whole.reshape(cells, lanes))
         head, tail = high[at], low[at]
         part[...] += transposed_dot(head, head)
         cross[...] += transposed_dot(head, tail)
@@ -290,6 +324,10 @@
         gather_cols(offset).wait_recv()
     for offset in range(1, n_space):
         gather_rows(offset).start()
+    for chunk in range(GATHERED):
+        for half in range(2):
+            if (half, chunk) != (0, 0):
+                gather_start(half, chunk)
     for offset in range(1, n_space):
         gather_rows(offset).wait_recv()
 
@@ -320,14 +358,39 @@
     fs = split(factor_of(product(zs, ys)))
     z_ref[...] = product(fs, zs) / jnp.sqrt(norm_scale)
 
-    @pl.loop(0, CHUNKS)
+    @pl.loop(GATHERED, CHUNKS)
     def _(chunk):
         at = pl.ds(pl.multiple_of(chunk * cells, cells), cells)
         value = product((high[at], low[at]), split(z_ref[...]))
-        white[chunk] = value.reshape(share, rows, nz, norb)
+        white[chunk - GATHERED] = value.reshape(share, rows, nz, norb)
         for offset in range(1, n_orb):
             back(chunk, offset).start()
         back_own_copy(chunk).start()
+
+    own = split(z_ref[:, lane_block(me_o)])
+
+    for chunk in range(GATHERED):
+        at = pl.ds(chunk * cells, cells)
+        ys = pl.ds(chunk * rows, rows)
+        value = product((high[at], low[at]), own)
+        out_ref[pl.ds(me_o * share, share), ys] = value.reshape(share, rows, nz, lanes)
+        for turn_at in range(1, n_orb):
+            owned = pl.ds(lax.rem(me_o + turn_at, n_orb) * share, share)
+            for half in range(2):
+                for offset in range(1, n_orb):
+                    gather(half, chunk, offset, turn_at).wait_recv()
+                extra[half, chunk, turn_at, :, :, :, lane_block(me_o)] = last[half, owned, ys]
+            parts = []
+            for block in range(n_orb):
+                columns = pl.ds(block * lanes, lanes)
+                parts.append(
+                    unpacked(
+                        extra[0, chunk, turn_at, :, :, :, columns],
+                        extra[1, chunk, turn_at, :, :, :, columns],
+                    )
+                )
+            field = tuple(jnp.concatenate([p[i] for p in parts], axis=1) for i in range(2))
+            out_ref[owned, ys] = product(field, own).reshape(share, rows, nz, lanes)
 
     for offset in range(1, n_space):
         send_rows(offset).wait_send()
@@ -345,10 +408,20 @@
 
     @pl.loop(0, CHUNKS)
     def _(chunk):
-        back_own_copy(chunk).wait()
         for offset in range(1, n_orb):
             outward(0, chunk, offset).wait_send()
             outward(1, chunk, offset).wait_send()
+
+    for chunk in range(GATHERED):
+        for half in range(2):
+            for turn_at in range(1, n_orb):
+                for offset in range(1, n_orb):
+                    gather(half, chunk, offset, turn_at).wait_send()
+
+    @pl.loop(GATHERED, CHUNKS)
+    def _(chunk):
+        back_own_copy(chunk).wait()
+        for offset in range(1, n_orb):
             back(chunk, offset).wait()
 
 
@@ -358,10 +431,8 @@
     piece = norb // n_space
     block = (CHUNKS, planes // n_orb, ny // CHUNKS, nz, norb)
     cells = planes * ny * nz // n_orb
-    coef = potential - (CENTER + 1.5 * STENCIL_WEIGHTS[0])
-    coef = jnp.swapaxes(coef.reshape(planes, ny, 2, nz // 2), 2, 3)
-    coef = jnp.broadcast_to(coef[..., None], coef.shape + (lanes // 2,))
-    coef = coef.reshape(planes, ny, nz // 2, lanes)
+    by_depth = jnp.transpose(potential.reshape(planes, ny, 2, nz // 2), (0, 3, 2, 1))
+    by_depth = by_depth.reshape(planes, nz // 2, 2 * ny)
     f32 = jnp.float32
     dma = pltpu.SemaphoreType.DMA
     return pl.pallas_call(
@@ -371,9 +442,11 @@
         out_specs=pl.BlockSpec(memory_space=pltpu.VMEM),
         scratch_shapes=[
             pltpu.VMEM((planes, ny, nz, lanes), f32),
+            pltpu.VMEM((planes, ny, nz // 2, lanes), f32),
             pltpu.VMEM((2, DEGREE, planes + 2 * REACH, ny, nz // 2, lanes), f32),
             pltpu.VMEM((2, planes, ny, nz // 2, lanes), f32),
             pltpu.VMEM((2,) + block[:3] + (nz // 2, norb), f32),
+            pltpu.VMEM((2, GATHERED, n_orb) + block[1:3] + (nz // 2, norb), f32),
             pltpu.VMEM((cells, norb), jnp.bfloat16),
             pltpu.VMEM((cells, norb), jnp.bfloat16),
             pltpu.VMEM((norb, norb), f32),
@@ -384,13 +457,15 @@
             pltpu.VMEM((norb, norb), f32),
             pltpu.VMEM((norb, norb), f32),
             pltpu.VMEM((norb, norb), f32),
-            pltpu.VMEM(block, f32),
+            pltpu.VMEM((CHUNKS - GATHERED,) + block[1:], f32),
             dma,
             dma((2, DEGREE, CHUNKS, 2)),
             dma((2, DEGREE, CHUNKS, 2)),
             dma((2, CHUNKS, n_orb)),
             dma((2, CHUNKS, n_orb)),
             dma((2, CHUNKS)),
+            dma((2, GATHERED, n_orb, n_orb)),
+            dma((2, GATHERED, n_orb, n_orb)),
             dma((n_space,)),
             dma((n_space,)),
             dma((n_orb,)),
@@ -409,7 +484,7 @@
         cost_estimate=pl.CostEstimate(
             flops=20_000_000_000, bytes_accessed=8_000_000, transcendentals=0
         ),
-    )(orbitals, coef)
+    )(orbitals, by_depth)
 
 
 def solution(mesh):

time: 214 us -> 216 us (level)
  Pallas kernels: 203 us -> 210 us
  local copies, waits for them, and re-layouts: 8.59 us -> 4.92 us
    pallas_call x1, Pallas kernels: 203 us -> 210 us  [body(): pl.pallas_call(functools.partial(kernel, n_space, n_orb), out_shape=jax.S...]
    broadcast_in_dim x1 -> x0, local copies, waits for them, and re-layouts: 2.43 us -> none  [body(): coef = jnp.broadcast_to(coef[..., None], coef.shape + (lanes // 2,))]
where the time goes in v4:
time: 216 us; the launch traced here: 215 us
  Pallas kernels  210 us (97%)
  local copies, waits for them, and re-layouts  4.92 us (2%)
    pallas_call x1, Pallas kernels, body(): pl.pallas_call(functools.partial(kernel, n_space, n_orb), out_shape=jax.S...  210 us

profile of v4, /device:TPU:0, one launch (start us, length us, event | category | flops | bytes accessed | tf_op | source)
XLA Modules:
  0.0 215.3 jit_solution(9439137627705238078)
XLA Ops:
  0.0 1.0 reshape.6
  1.0 0.1 copy.3
  1.1 0.8 reshape.7.potential_ref
  1.9 210.4 %shard_map.28 = f32[8,16,32,128]{3,2,1,0:T(8,128)} custom-call(f32[8,16,32,128]{3,2,1,0:T(8,128)} %x_ref.1, f32[8,16,32]{2,1,0:T(8,128)} %reshape.7.potential_ref), custom_call_target="tpu_custom_call" | custom-call | flops 20000000000 | bytes 8000000 | tf_op jit(solution)/shard_map/pallas_call | solution.py:438
  212.2 3.1 %copy.5 = f32[8,16,32,128]{3,2,1,0:T(8,128)} copy(f32[8,16,32,128]{3,2,1,0:T(8,128)} %shard_map.28) | data formatting | bytes 4194304

commit v5 on v4

--- a/solution.py
+++ b/solution.py
@@ -15,7 +15,7 @@
 HALF_WIDTH = 4.0
 REACH = 3
 CHUNKS = 4
-GATHERED = 2
+GATHERED = 1
 MESH = pl.DeviceIdType.MESH
 
 
@@ -41,8 +41,9 @@
 
 def kernel(
     n_space, n_orb, x_ref, potential_ref, out_ref,
-    raw, coef_ref, fields, last, mixed, extra, high, low, part, cross, landed, summed, landed_cols, total, y_ref, z_ref, white,
+    raw, coef_ref, fields, last, mixed, extra, high, low, part, cross, landed_half, landed, summed, landed_cols, total, y_ref, z_ref, white,
     load_sem, halo_send, halo_recv, to_send, to_recv, to_own, extra_send, extra_recv,
+    half_send, half_recv, ghalf_send, ghalf_recv,
     rows_send, rows_recv, cols_send, cols_recv, gcols_send, gcols_recv, grows_send, grows_recv,
     back_send, back_recv, back_own,
 ):
@@ -65,8 +66,15 @@
     def orb_peer(offset):
         return lax.rem(me_o + offset, n_orb)
 
-    def row_block(device):
-        return pl.ds(pl.multiple_of(device * piece, piece), piece)
+    n_pair = n_space // 2
+    core = lax.rem(me_s, 2)
+    pair = me_s // 2
+
+    def core_rows(at):
+        return pl.ds(pl.multiple_of(at * (n_pair * piece), n_pair * piece), n_pair * piece)
+
+    def row_block(at):
+        return pl.ds(pl.multiple_of((core * n_pair + at) * piece, piece), piece)
 
     def lane_block(device):
         return pl.ds(pl.multiple_of(device * lanes, lanes), lanes)
@@ -250,8 +258,6 @@
     for step in range(1, DEGREE):
         filter_step(1, step)
 
-    gather_start(0, 0)
-
     def unpacked(one, two):
         shape = (share * rows, deep, lanes)
         one, two = one.reshape(shape), two.reshape(shape)
@@ -282,11 +288,19 @@
 
     part[...] = (part[...] + 2.0 * cross[...]) * (1.0 / (CHUNKS * cells * n_space * n_orb))
 
+    def pair_peer(offset):
+        return lax.rem(pair + offset, n_pair)
+
+    def send_half():
+        return remote(
+            part.at[core_rows(1 - core)], landed_half, half_send, half_recv, 2 * pair + 1 - core, me_o
+        )
+
     def send_rows(offset):
-        peer = space_peer(offset)
+        peer = pair_peer(offset)
         return remote(
             part.at[row_block(peer)], landed.at[offset - 1],
-            rows_send.at[offset], rows_recv.at[offset], peer, me_o,
+            rows_send.at[offset], rows_recv.at[offset], 2 * peer + core, me_o,
         )
 
     def send_cols(offset):
@@ -297,17 +311,26 @@
         )
 
     def gather_cols(offset):
-        block = total.at[row_block(me_s), lane_block(me_o)]
+        block = total.at[row_block(pair), lane_block(me_o)]
         return remote(block, block, gcols_send.at[offset], gcols_recv.at[offset], me_s, orb_peer(offset))
 
     def gather_rows(offset):
-        block = total.at[row_block(me_s)]
-        return remote(block, block, grows_send.at[offset], grows_recv.at[offset], space_peer(offset), me_o)
-
-    for offset in range(1, n_space):
+        block = total.at[row_block(pair)]
+        return remote(
+            block, block, grows_send.at[offset], grows_recv.at[offset], 2 * pair_peer(offset) + core, me_o
+        )
+
+    def gather_half():
+        block = total.at[core_rows(core)]
+        return remote(block, block, ghalf_send, ghalf_recv, 2 * pair + 1 - core, me_o)
+
+    send_half().start()
+    send_half().wait_recv()
+    part[core_rows(core)] += landed_half[...]
+    for offset in range(1, n_pair):
         send_rows(offset).start()
-    value = part[row_block(me_s)]
-    for offset in range(1, n_space):
+    value = part[row_block(pair)]
+    for offset in range(1, n_pair):
         send_rows(offset).wait_recv()
         value = value + landed[offset - 1]
     summed[...] = value
@@ -317,19 +340,20 @@
     for offset in range(1, n_orb):
         send_cols(offset).wait_recv()
         value = value + landed_cols[offset - 1]
-    total[row_block(me_s), lane_block(me_o)] = value
+    total[row_block(pair), lane_block(me_o)] = value
     for offset in range(1, n_orb):
         gather_cols(offset).start()
     for offset in range(1, n_orb):
         gather_cols(offset).wait_recv()
-    for offset in range(1, n_space):
+    for offset in range(1, n_pair):
         gather_rows(offset).start()
     for chunk in range(GATHERED):
         for half in range(2):
-            if (half, chunk) != (0, 0):
-                gather_start(half, chunk)
-    for offset in range(1, n_space):
+            gather_start(half, chunk)
+    for offset in range(1, n_pair):
         gather_rows(offset).wait_recv()
+    gather_half().start()
+    gather_half().wait_recv()
 
     one_sided = total[...]
     intersection = 0.5 * (one_sided + one_sided.T)
@@ -392,7 +416,9 @@
             field = tuple(jnp.concatenate([p[i] for p in parts], axis=1) for i in range(2))
             out_ref[owned, ys] = product(field, own).reshape(share, rows, nz, lanes)
 
-    for offset in range(1, n_space):
+    send_half().wait_send()
+    gather_half().wait_send()
+    for offset in range(1, n_pair):
         send_rows(offset).wait_send()
         gather_rows(offset).wait_send()
     for offset in range(1, n_orb):
@@ -451,7 +477,8 @@
             pltpu.VMEM((cells, norb), jnp.bfloat16),
             pltpu.VMEM((norb, norb), f32),
             pltpu.VMEM((norb, norb), f32),
-            pltpu.VMEM((n_space - 1, piece, norb), f32),
+            pltpu.VMEM((norb // 2, norb), f32),
+            pltpu.VMEM((n_space // 2 - 1, piece, norb), f32),
             pltpu.VMEM((piece, norb), f32),
             pltpu.VMEM((n_orb - 1, piece, lanes), f32),
             pltpu.VMEM((norb, norb), f32),
@@ -466,14 +493,18 @@
             dma((2, CHUNKS)),
             dma((2, GATHERED, n_orb, n_orb)),
             dma((2, GATHERED, n_orb, n_orb)),
-            dma((n_space,)),
-            dma((n_space,)),
+            dma,
+            dma,
+            dma,
+            dma,
+            dma((n_space // 2,)),
+            dma((n_space // 2,)),
             dma((n_orb,)),
             dma((n_orb,)),
             dma((n_orb,)),
             dma((n_orb,)),
-            dma((n_space,)),
-            dma((n_space,)),
+            dma((n_space // 2,)),
+            dma((n_space // 2,)),
             dma((CHUNKS, n_orb)),
             dma((CHUNKS, n_orb)),
             dma((CHUNKS,)),

time: 216 us -> 198 us (0.917)
  Pallas kernels: 210 us -> 193 us
    pallas_call x1, Pallas kernels: 210 us -> 193 us  [body(): pl.pallas_call(functools.partial(kernel, n_space, n_orb), out_shape=jax.S...]
where the time goes in v5:
time: 198 us
  Pallas kernels  193 us (97%)
  local copies, waits for them, and re-layouts  4.92 us (2%)
    pallas_call x1, Pallas kernels, body(): pl.pallas_call(functools.partial(kernel, n_space, n_orb), out_shape=jax.S...  193 us

profile of v5, /device:TPU:0, one launch (start us, length us, event | category | flops | bytes accessed | tf_op | source)
XLA Modules:
  0.0 197.9 jit_solution(11245610041079497634)
XLA Ops:
  0.0 1.0 reshape.6
  1.0 0.1 copy.3
  1.1 0.8 reshape.7.potential_ref
  1.9 193.0 %shard_map.28 = f32[8,16,32,128]{3,2,1,0:T(8,128)} custom-call(f32[8,16,32,128]{3,2,1,0:T(8,128)} %x_ref.1, f32[8,16,32]{2,1,0:T(8,128)} %reshape.7.potential_ref), custom_call_target="tpu_custom_call" | custom-call | flops 20000000000 | bytes 8000000 | tf_op jit(solution)/shard_map/pallas_call | solution.py:464
  194.9 3.1 %copy.5 = f32[8,16,32,128]{3,2,1,0:T(8,128)} copy(f32[8,16,32,128]{3,2,1,0:T(8,128)} %shard_map.28) | data formatting | bytes 4194304

commit v6 on v5

--- a/solution.py
+++ b/solution.py
@@ -167,13 +167,16 @@
     def turned(value):
         return pltpu.roll(value, turn, value.ndim - 1)
 
-    @pl.loop(0, planes)
-    def _(plane):
-        @pl.loop(0, ny)
-        def _(y):
-            top, bottom = raw[plane, y, :deep], raw[plane, y, deep:]
-            fields[0, 0, plane + REACH, y] = jnp.where(first_lanes, top, turned(bottom))
-            fields[1, 0, plane + REACH, y] = jnp.where(first_lanes, turned(top), bottom)
+    def pack(half):
+        @pl.loop(0, planes)
+        def _(plane):
+            for y in range(ny):
+                top, bottom = raw[plane, y, :deep], raw[plane, y, deep:]
+                if half == 0:
+                    value = jnp.where(first_lanes, top, turned(bottom))
+                else:
+                    value = jnp.where(first_lanes, turned(top), bottom)
+                fields[half, 0, plane + REACH, y] = value
 
     def send_halos(half, step):
         @pl.loop(0, CHUNKS)
@@ -210,7 +213,7 @@
             halo(half, step, chunk, 0).wait_recv()
             halo(half, step, chunk, 1).wait_recv()
 
-            @pl.loop(0, planes)
+            @pl.loop(0, planes, unroll=2)
             def _(plane):
                 at = plane + REACH
                 for row in range(rows):
@@ -239,7 +242,9 @@
                     outward(half, chunk, offset).start()
                 outward_own(half, chunk).start()
 
+    pack(0)
     send_halos(0, 0)
+    pack(1)
 
     @pl.loop(0, planes)
     def _(plane):

time: 198 us -> 190 us (0.960)
  Pallas kernels: 193 us -> 184 us
    pallas_call x1, Pallas kernels: 193 us -> 184 us  [body(): pl.pallas_call(functools.partial(kernel, n_space, n_orb), out_shape=jax.S...]
where the time goes in v6:
time: 190 us; the launch traced here: 189 us
  Pallas kernels  184 us (97%)
  local copies, waits for them, and re-layouts  4.92 us (3%)
    pallas_call x1, Pallas kernels, body(): pl.pallas_call(functools.partial(kernel, n_space, n_orb), out_shape=jax.S...  184 us

profile of v6, /device:TPU:0, one launch (start us, length us, event | category | flops | bytes accessed | tf_op | source)
XLA Modules:
  0.0 189.4 jit_solution(4253250223302279919)
XLA Ops:
  0.0 1.0 reshape.6
  1.0 0.1 copy.3
  1.1 0.8 reshape.7.potential_ref
  1.9 184.4 %shard_map.28 = f32[8,16,32,128]{3,2,1,0:T(8,128)} custom-call(f32[8,16,32,128]{3,2,1,0:T(8,128)} %x_ref.1, f32[8,16,32]{2,1,0:T(8,128)} %reshape.7.potential_ref), custom_call_target="tpu_custom_call" | custom-call | flops 20000000000 | bytes 8000000 | tf_op jit(solution)/shard_map/pallas_call | solution.py:469
  186.3 3.1 %copy.5 = f32[8,16,32,128]{3,2,1,0:T(8,128)} copy(f32[8,16,32,128]{3,2,1,0:T(8,128)} %shard_map.28) | data formatting | bytes 4194304
